TPU v7x, 512 devices: a whole 4x8x8 slice. The times are simulated.
512 devices in a mesh: node: 32 (over x, y), chan: 16 (over z, core).
Axes of the slice: x: 4, y: 8, z: 8, core: 2. Of those that a mesh axis runs over, the one named last changes fastest.
Arguments:
- features: bfloat16 [57344, 1024], P('node', 'chan'), may hold values from -0.046875 to 0.046875
- weight: bfloat16 [1024, 1024], P('node', 'chan'), may hold values from -0.375 to 0.375
- pre_clean: bfloat16 [57344, 1024], P('node', 'chan'), may hold values from -6 to 6
- pre_corrupt: bfloat16 [57344, 1024], P('node', 'chan'), may hold values from -6 to 6
- grad_clean: bfloat16 [57344, 1024], P('node', 'chan'), may hold values from -6 to 6
- grad_corrupt: bfloat16 [57344, 1024], P('node', 'chan'), may hold values from -6 to 6
- slopes: float32 [1024], P('chan'), may hold values from 0.05 to 0.5
- adj_vals: bfloat16 [448, 5, 128, 128], P('node'), may hold values from 0 to 0.07861328
- adj_cols: int32 [448, 5], P('node'), may hold values from 0 to 447, as said below
- adj_count: int32 [448], P('node'), may hold values from 1 to 5, as said below
- shuffle_from: int32 [448], replicated, may hold values from 0 to 447, as said below
Outputs:
- grad_weight: float32 [1024, 1024], P('node', 'chan')
- grad_features: bfloat16 [57344, 1024], P('node', 'chan')
Inputs may be any that keep to these rules, and one draw needn't show every extreme that they name: `adj_cols`: entry [b, k] is a block within 2 of b, and entry [b, 0] is b itself. Slots k < adj_count[b] of row block b hold edge tiles; the other slots are padding and are not read. `shuffle_from`: A permutation of the blocks. The 14 blocks of one index of node take their rows from exactly 14 distinct indices of node, 1 block from each; among these are the index just after it and the index 16 away, counted round.
All inputs are finite; a program needn't handle non-finite values.
Results may differ from a plain program's by a relative error of at most 0.023.
Values may be sent and summed in bfloat16 or wider, within the bound.
A program may use at most 64 MiB of HBM per device.

v0:
```python
import jax
import jax.numpy as jnp
from jax import lax
from jax.sharding import PartitionSpec as P


def shifted(value, axis, by):
    size = lax.axis_size(axis)
    pairs = [(i, i + by) for i in range(size) if 0 <= i + by < size]
    return lax.ppermute(value, axis, pairs)


def local_grad(grad_part, pre_part, slopes):
    factor = jnp.where(pre_part > 0, 1.0, slopes[None, :])
    return (grad_part.astype(jnp.float32) * factor).astype(jnp.bfloat16)


def local(
    features,
    weight,
    pre_clean,
    pre_corrupt,
    grad_clean,
    grad_corrupt,
    slopes,
    adj_vals,
    adj_cols,
    adj_count,
    shuffle_from,
):
    row_count, chan_width = features.shape
    blocks = adj_vals.shape[0]
    tile_slots = adj_vals.shape[1]
    tile_rows = adj_vals.shape[2]
    band_reach = (tile_slots - 1) // 2
    my_index = lax.axis_index("node")
    dev_count = lax.axis_size("node")
    d_clean = local_grad(grad_clean, pre_clean, slopes)
    d_corrupt = local_grad(grad_corrupt, pre_corrupt, slopes)
    stacked = jnp.concatenate([d_clean, d_corrupt], axis=1).reshape(
        blocks, tile_rows, 2 * chan_width
    )
    contrib = jnp.einsum("bkpq,bpc->bkqc", adj_vals, stacked, preferred_element_type=jnp.float32)
    span_blocks = blocks + 2 * band_reach
    targets = adj_cols - (my_index * blocks - band_reach)
    live_mask = jnp.arange(tile_slots)[None, :] < adj_count[:, None]
    chooser = (
        (targets.reshape(-1)[None, :] == jnp.arange(span_blocks)[:, None])
        & live_mask.reshape(-1)[None, :]
    ).astype(jnp.float32)
    summed = jnp.dot(
        chooser, contrib.reshape(blocks * tile_slots, -1), precision=lax.Precision.HIGHEST
    )
    summed = summed.reshape(span_blocks, tile_rows, 2 * chan_width)
    from_prev = shifted(summed[band_reach + blocks :].astype(jnp.bfloat16), "node", 1).astype(
        jnp.float32
    )
    from_next = shifted(summed[:band_reach].astype(jnp.bfloat16), "node", -1).astype(jnp.float32)
    remaining = blocks - band_reach
    middle = summed[band_reach : band_reach + blocks]
    middle = (
        middle
        + jnp.pad(from_prev, ((0, remaining), (0, 0), (0, 0)))
        + jnp.pad(from_next, ((remaining, 0), (0, 0), (0, 0)))
    )
    backprop = middle.astype(jnp.bfloat16).reshape(row_count, 2 * chan_width)
    back_clean = backprop[:, :chan_width]
    back_corrupt = backprop[:, chan_width:]
    my_blocks = my_index * blocks + jnp.arange(blocks)
    all_blocks = jnp.arange(shuffle_from.shape[0])
    one_hot = (shuffle_from[None, :] == my_blocks[:, None]).astype(jnp.int32)
    source_block = jnp.sum(one_hot * all_blocks[None, :], axis=1)
    wanted = (source_block[:, None] * tile_rows + jnp.arange(tile_rows)[None, :]).reshape(-1)
    portion = lax.all_gather(back_corrupt, "node", axis=0, tiled=True)
    inside = (wanted >= 0) & (wanted < portion.shape[0])
    fetched = jnp.take(portion, jnp.clip(wanted, 0, portion.shape[0] - 1), axis=0)
    unshuffled = jnp.where(inside[:, None], fetched, jnp.zeros_like(back_corrupt))
    combined = jnp.concatenate([back_clean, unshuffled], axis=1)
    product = lax.dot_general(
        lax.all_gather(features, "chan", axis=1, tiled=True),
        combined,
        (((0,), (0,)), ((), ())),
        preferred_element_type=jnp.float32,
    )
    partial_w = product[:, :chan_width] + product[:, chan_width:]
    share_rows = partial_w.shape[0] // dev_count
    summed_w = lax.psum(partial_w.astype(jnp.bfloat16), "node").astype(jnp.float32)
    grad_weight = lax.dynamic_slice_in_dim(summed_w, my_index * share_rows, share_rows, 0)
    portion = lax.all_gather(weight, "node", axis=0, tiled=True)
    doubled = jnp.concatenate([portion, portion], axis=1)
    partial_x = lax.dot_general(
        combined, doubled, (((1,), (1,)), ((), ())), preferred_element_type=jnp.float32
    )
    grad_features = lax.psum_scatter(
        partial_x.astype(jnp.bfloat16), "chan", scatter_dimension=1, tiled=True
    )
    return (grad_weight, grad_features)


def solution(mesh):
    placed = (
        P("node", "chan"),
        P("node", "chan"),
        P("node", "chan"),
        P("node", "chan"),
        P("node", "chan"),
        P("node", "chan"),
        P("chan"),
        P("node", None, None, None),
        P("node", None),
        P("node"),
        P(),
    )
    return jax.shard_map(
        local,
        mesh=mesh,
        in_specs=placed,
        out_specs=(P("node", "chan"), P("node", "chan")),
        check_vma=False,
    )
```

profile of v0, /device:TPU:2, one launch (start us, length us, event | category | flops | bytes accessed | tf_op | source)
XLA Modules:
  0.0 460.4 jit_solution(3532302501971480463)
XLA Ops:
  7.2 0.0 copy-start
  7.2 0.0 all-gather.3.cloned.1.call-start
  7.2 1.4 copy.28
  8.6 1.2 copy.29
  9.8 1.9 copy.30
  11.7 1.9 copy.31
  13.6 1.5 multiply_convert_fusion.1
  15.2 0.3 pad_maximum_fusion
  15.4 2.9 convolution_bitcast_fusion
  18.3 5.7 %copy.33 = f32[14,5,128,128]{3,2,1,0:T(8,128)} copy(f32[14,5,128,128]{2,3,1,0:T(8,128)} %convolution_bitcast_fusion) | data formatting | bytes 9175040 | tf_op jit(solution)/shard_map/bkpq,bpc->bkqc/dot_general | solution.py:43
  24.1 2.9 pad.25
  27.0 4.9 %copy.38 = f32[9,8,128,128]{3,1,2,0:T(8,128)} copy(f32[9,8,128,128]{3,2,1,0:T(8,128)S(1)} %bitcast.49) | data formatting | bytes 9437184
  31.9 0.1 copy.27
  32.0 0.1 eq.28
  32.1 0.1 iota_compare_fusion.1
  32.2 0.1 lt.58
  32.3 4.1 fusion.24
  36.4 0.1 slice_bitcast_fusion.1
  36.5 3.5 collective-permute-start
  40.0 4.5 collective-permute-start.1
  44.5 0.1 slice.38
  44.6 0.2 copy.39
  44.8 1.5 collective-permute-done.1
  46.3 0.1 fusion.1
  46.4 1.0 fusion.23
  47.4 0.0 all-gather.3.cloned.1.call-update
  47.4 0.0 all-gather.5.cloned.1.call-start
  47.4 0.7 all-gather.5.cloned.1.call-update
  48.2 0.0 all-reduce.4.cloned.1.call-start
  48.2 50.6 %all_gather.11 = bf16[1024,64]{1,0:T(8,128)(2,1)S(1)} all-gather(bf16[32,64]{1,0:T(8,128)(2,1)S(1)} %copy-done.1), channel_id=1, replica_groups=mesh['node'=32,'chan'=16] {'node'}, dimensions={0}, use_global_device_ids=true | all-gather | bytes 135168 | tf_op jit(solution)/shard_map/all_gather | solution.py:89
  98.8 0.2 select_reduce_fusion
  99.0 0.1 fusion.12
  99.1 0.1 fusion.15
  99.2 0.1 fusion.17
  99.3 86.6 %all-gather.3.cloned.1.call-done = bf16[57344,64]{1,0:T(8,128)(2,1)} async-done(((bf16[1792,64]{1,0:T(8,128)(2,1)}), bf16[57344,64]{1,0:T(8,128)(2,1)}) %all-gather.3.cloned.1.call-update) | async-done | bytes 7340048 | tf_op jit(solution)/shard_map/all_gather | solution.py:74
  185.9 11.3 %gather_fusion = bf16[1792,64]{1,0:T(8,128)(2,1)} fusion(bf16[57344,64]{1,0:T(8,128)(2,1)} %all-gather.3.cloned.1.call-done, s32[2048]{0:T(1024)S(1)} %pad_clamp_fusion), kind=kCustom, calls=%fused_computation | custom fusion | bytes 465920 | tf_op jit(solution)/shard_map/jit(_take)/gather | solution.py:76
  197.1 2.7 select_select_fusion
  199.8 32.0 %all-gather.5.cloned.1.call-done = bf16[1792,1024]{0,1:T(8,128)(2,1)} async-done(((bf16[1792,64]{0,1:T(8,128)(2,1)}), bf16[1792,1024]{0,1:T(8,128)(2,1)}) %all-gather.5.cloned.1.call-update) | async-done | bytes 3670032 | tf_op jit(solution)/shard_map/all_gather | solution.py:80
  231.8 3.7 convolution_bitcast_fusion.1
  235.5 0.7 fusion.2
  236.1 0.0 all-reduce.4.cloned.1.call-update
  236.2 0.0 reduce-scatter.2.cloned.1.call-start
  236.2 3.0 convolution_convert_fusion
  239.2 0.0 reduce-scatter.2.cloned.1.call-update
  239.3 147.1 %all-reduce.4.cloned.1.call-done = bf16[1024,64]{0,1:T(8,128)(2,1)} async-done(((bf16[1024,64]{0,1:T(8,128)(2,1)}), bf16[1024,64]{0,1:T(8,128)(2,1)}) %all-reduce.4.cloned.1.call-update) | async-done | bytes 131088 | tf_op jit(solution)/shard_map/psum | solution.py:87
  386.4 0.8 dynamic-slice_convert_fusion
  387.2 0.7 copy.34
  387.9 66.0 %reduce-scatter.2.cloned.1.call-done = bf16[1792,64]{0,1:T(8,128)(2,1)} async-done(((bf16[1792,1024]{0,1:T(8,128)(2,1)}), bf16[1792,64]{0,1:T(8,128)(2,1)}) %reduce-scatter.2.cloned.1.call-update) | async-done | bytes 229392 | tf_op jit(solution)/shard_map/reduce_scatter | solution.py:94
  (17 shorter events, 0.1 us)
Async XLA Ops:
  7.2 8.3 %copy-start = (bf16[14,5,128,128]{3,2,1,0:T(8,128)(2,1)S(1)}, bf16[14,5,128,128]{3,2,1,0:T(8,128)(2,1)}, u32[]{:S(2)}) copy-start(bf16[14,5,128,128]{3,2,1,0:T(8,128)(2,1)} %param.18) | copy-start | bytes 6881284
  7.2 178.7 %all-gather.3.cloned.1.call-start = ((), (), s32[]{:S(2)}) async-start(), calls=%async_computation.1 | async-start | bytes 15138816 | tf_op jit(solution)/shard_map/all_gather | solution.py:74
  27.0 4.9 %copy-start.2 = (s32[14,5]{0,1:T(8,128)S(1)}, s32[14,5]{0,1:T(8,128)}, u32[]{:S(2)}) copy-start(s32[14,5]{0,1:T(8,128)} %param.19) | copy-start | bytes 844
  27.0 5.1 %copy-start.4 = (s32[14]{0:T(128)S(1)}, s32[14]{0:T(128)}, u32[]{:S(2)}) copy-start(s32[14]{0:T(128)} %param.20) | copy-start | bytes 172
  36.5 8.3 %collective-permute-start = (bf16[2,128,128]{2,1,0:T(8,128)(2,1)S(1)}, bf16[2,128,128]{2,1,0:T(8,128)(2,1)S(1)}, u32[]{:S(2)}, u32[]{:S(2)}) collective-permute-start(bf16[2,128,128]{2,1,0:T(8,128)(2,1)S(1)} %bitcast.56), channel_id=1, source_target_pairs={{0,16},{16,32},{32,48},{48,64},{64,80},{80,96},{96,112},{112,128},... | collective-permute-start | bytes 196616 | tf_op jit(solution)/shard_map/ppermute | solution.py:10
  40.0 6.4 %collective-permute-start.1 = (bf16[2,128,128]{2,1,0:T(8,128)(2,1)S(1)}, bf16[2,128,128]{2,1,0:T(8,128)(2,1)S(1)}, u32[]{:S(2)}, u32[]{:S(2)}) collective-permute-start(bf16[2,128,128]{2,1,0:T(8,128)(2,1)S(1)} %bitcast.57), channel_id=1, source_target_pairs={{16,0},{32,16},{48,32},{64,48},{80,64},{96,80},{112,96},{128,112},... | collective-permute-start | bytes 196616 | tf_op jit(solution)/shard_map/ppermute | solution.py:10
  44.4 3.8 copy-start.1
  44.6 54.2 %copy-start.3 = (s32[448]{0:T(512)S(1)}, s32[448]{0:T(512)}, u32[]{:S(2)}) copy-start(s32[448]{0:T(512)} %param.21) | copy-start | bytes 5380
  47.4 184.4 %all-gather.5.cloned.1.call-start = ((), (), s32[]{:S(2)}) async-start(), calls=%async_computation.2 | async-start | bytes 3899392 | tf_op jit(solution)/shard_map/all_gather | solution.py:80
  48.2 338.2 %all-reduce.4.cloned.1.call-start = ((), (), s32[]{:S(2)}) async-start(), calls=%async_computation.3 | async-start | bytes 262144 | tf_op jit(solution)/shard_map/psum | solution.py:87
  236.2 217.7 %reduce-scatter.2.cloned.1.call-start = ((), (), s32[]{:S(2)}) async-start(), calls=%async_computation.4 | async-start | bytes 3899392 | tf_op jit(solution)/shard_map/reduce_scatter | solution.py:94
Sparse Core Ops, SparseCore 0:
  47.5 138.3 all-gather.2
  188.0 43.7 all-gather.4
  236.3 150.0 all-reduce.3
  389.9 63.8 reduce-scatter.1
where the time goes:
time: 461 us; the launch traced here: 460 us
  waiting for transfers between devices  334 us (72%)
  blocking collectives  50.6 us (11%)
  local copies, waits for them, and re-layouts  33.5 us (7%)
  between operations  14 us (3%)
  matrix products  13.7 us (3%)
  starting transfers between devices  8.11 us (2%)
  other arithmetic  6.56 us (1%)
    psum x1, waiting for transfers between devices, local(): lax.psum(partial_w.astype(jnp.bfloat16), 'node').astype(jnp.float32)  147 us
    all_gather x1, waiting for transfers between devices, local(): portion = lax.all_gather(back_corrupt, 'node', axis=0, tiled=True)  86.6 us
    reduce_scatter x1, waiting for transfers between devices, local(): lax.psum_scatter(partial_x.astype(jnp.bfloat16), 'chan', scatter_dimensio...  66 us
    all_gather x1, blocking collectives, local(): portion = lax.all_gather(weight, 'node', axis=0, tiled=True)  50.6 us
    all_gather x1, waiting for transfers between devices, local(): lax.all_gather(features, 'chan', axis=1, tiled=True)  32 us
    unnamed x21, local copies, waits for them, and re-layouts  15.2 us
    gather x1, local copies, waits for them, and re-layouts, local(): jnp.take(portion, jnp.clip(wanted, 0, portion.shape[0] - 1), axis=0)  11.3 us
  transfers between devices with their start and end apart: 6, of which 5 were waited for; matrix products, arithmetic and copies ran while one was open for 4% of the time, Pallas kernels for 0%

commit v1 on v0

--- a/solution.py
+++ b/solution.py
@@ -71,7 +71,9 @@
     one_hot = (shuffle_from[None, :] == my_blocks[:, None]).astype(jnp.int32)
     source_block = jnp.sum(one_hot * all_blocks[None, :], axis=1)
     wanted = (source_block[:, None] * tile_rows + jnp.arange(tile_rows)[None, :]).reshape(-1)
-    portion = lax.all_gather(back_corrupt, "node", axis=0, tiled=True)
+    portion = jnp.concatenate(
+        lax.all_to_all(jnp.stack([back_corrupt] * lax.axis_size("node")), "node", 0, 0), axis=0
+    )
     inside = (wanted >= 0) & (wanted < portion.shape[0])
     fetched = jnp.take(portion, jnp.clip(wanted, 0, portion.shape[0] - 1), axis=0)
     unshuffled = jnp.where(inside[:, None], fetched, jnp.zeros_like(back_corrupt))

time: 461 us -> 524 us (1.14)
  blocking collectives: 50.6 us -> 201 us
  waiting for transfers between devices: 334 us -> 221 us
  local copies, waits for them, and re-layouts: 33.5 us -> 49.5 us
  starting transfers between devices: 8.11 us -> 18.5 us
    all_gather x1, blocking collectives: 50.6 us -> 201 us  [local(): portion = lax.all_gather(weight, 'node', axis=0, tiled=True)]
    all_gather x1 -> x0, waiting for transfers between devices: 86.6 us -> none  [local(): portion = lax.all_gather(back_corrupt, 'node', axis=0, tiled=True)]
    all_gather x1, waiting for transfers between devices: 32 us -> 0.02 us  [local(): lax.all_gather(features, 'chan', axis=1, tiled=True)]
    all_to_all x0 -> x1, local copies, waits for them, and re-layouts: none -> 13.8 us  [local(): lax.all_to_all(jnp.stack([back_corrupt] * lax.axis_size('node')), 'node',...]
    all_to_all x0 -> x1, starting transfers between devices: none -> 10.4 us  [local(): lax.all_to_all(jnp.stack([back_corrupt] * lax.axis_size('node')), 'node',...]
    psum x1, waiting for transfers between devices: 147 us -> 153 us  [local(): lax.psum(partial_w.astype(jnp.bfloat16), 'node').astype(jnp.float32)]
    unnamed x21 -> x23, local copies, waits for them, and re-layouts: 15.2 us -> 15.2 us
  transfers between devices with their start and end apart: 6 -> 6, of which waited for: 5 -> 3; matrix products, arithmetic and copies ran while one was open for 4% -> 6% of each run, Pallas kernels for 0% -> 0%
where the time goes in v1:
time: 524 us; the launch traced here: 523 us
  waiting for transfers between devices  221 us (42%)
  blocking collectives  201 us (38%)
  local copies, waits for them, and re-layouts  49.5 us (9%)
  starting transfers between devices  18.5 us (4%)
  between operations  14 us (3%)
  matrix products  13.6 us (3%)
    all_gather x1, blocking collectives, local(): portion = lax.all_gather(weight, 'node', axis=0, tiled=True)  201 us
    psum x1, waiting for transfers between devices, local(): lax.psum(partial_w.astype(jnp.bfloat16), 'node').astype(jnp.float32)  153 us
    reduce_scatter x1, waiting for transfers between devices, local(): lax.psum_scatter(partial_x.astype(jnp.bfloat16), 'chan', scatter_dimensio...  66.2 us
    unnamed x23, local copies, waits for them, and re-layouts  15.2 us
    all_to_all x1, local copies, waits for them, and re-layouts, local(): lax.all_to_all(jnp.stack([back_corrupt] * lax.axis_size('node')), 'node',...  13.8 us
  transfers between devices with their start and end apart: 6, of which 3 were waited for; matrix products, arithmetic and copies ran while one was open for 6% of the time, Pallas kernels for 0%

profile of v1, /device:TPU:2, one launch (start us, length us, event | category | flops | bytes accessed | tf_op | source)
XLA Modules:
  0.0 523.0 jit_solution(9627198795274700671)
XLA Ops:
  7.2 1.4 copy.38
  8.5 1.2 copy.39
  9.8 1.9 copy.40
  11.7 1.9 copy.41
  13.6 1.5 multiply_convert_fusion.1
  15.1 0.3 pad_maximum_fusion
  15.4 2.9 convolution_bitcast_fusion
  18.3 5.7 %copy.43 = f32[14,5,128,128]{3,2,1,0:T(8,128)} copy(f32[14,5,128,128]{2,3,1,0:T(8,128)} %convolution_bitcast_fusion) | data formatting | bytes 9175040 | tf_op jit(solution)/shard_map/bkpq,bpc->bkqc/dot_general | solution.py:43
  24.0 2.9 pad.25
  27.0 4.9 copy.50
  31.8 0.1 copy.37
  31.9 0.1 eq.28
  32.0 0.1 iota_compare_fusion.1
  32.1 0.1 lt.58
  32.2 4.0 fusion.24
  36.3 0.1 slice_bitcast_fusion.1
  36.4 3.5 collective-permute-start
  39.9 4.5 collective-permute-start.1
  44.3 0.1 slice.38
  44.4 0.2 copy.51
  44.7 1.6 collective-permute-done.1
  46.2 0.1 fusion.1
  46.3 0.2 fusion.23
  46.5 0.2 copy.44
  46.7 3.8 stack.2
  50.5 10.4 %all-to-all-start = ((bf16[32,1792,64]{1,2,0:T(8,128)(2,1)}), bf16[32,1792,64]{1,2,0:T(8,128)(2,1)}, u32[]{:S(2)}, u32[]{:S(2)}) async-start(bf16[32,1792,64]{1,2,0:T(8,128)(2,1)} %stack.2), calls=%async_computation | async-start | bytes 14680064 | tf_op jit(solution)/shard_map/all_to_all | solution.py:75
  60.9 0.0 all-gather.2.cloned.1.call-start
  61.0 0.7 all-gather.2.cloned.1.call-update
  61.7 0.0 all-reduce.4.cloned.1.call-start
  61.7 200.8 %all_gather.7 = bf16[1024,64]{1,0:T(8,128)(2,1)S(1)} all-gather(bf16[32,64]{1,0:T(8,128)(2,1)S(1)} %copy-done.2), channel_id=1, replica_groups=mesh['node'=32,'chan'=16] {'node'}, dimensions={0}, use_global_device_ids=true | all-gather | bytes 135168 | tf_op jit(solution)/shard_map/all_gather | solution.py:91
  262.5 0.2 select_reduce_fusion
  262.7 0.1 fusion.12
  262.9 0.1 fusion.15
  262.9 0.1 fusion.17
  263.0 13.8 %copy.45 = bf16[32,1792,64]{2,1,0:T(8,128)(2,1)} copy(bf16[32,1792,64]{1,2,0:T(8,128)(2,1)} %all-to-all-done) | data formatting | bytes 14680064 | tf_op jit(solution)/shard_map/all_to_all | solution.py:75
  276.9 10.2 %gather_fusion = bf16[1792,64]{1,0:T(8,128)(2,1)S(1)} fusion(bf16[57344,64]{1,0:T(8,128)(2,1)} %bitcast.50, s32[2048]{0:T(1024)S(1)} %pad_clamp_fusion), kind=kCustom, calls=%fused_computation | custom fusion | bytes 465920 | tf_op jit(solution)/shard_map/jit(_take)/gather | solution.py:78
  287.1 1.3 select_select_fusion
  288.4 0.0 all-gather.2.cloned.1.call-done
  288.4 3.7 convolution_bitcast_fusion.1
  292.1 0.7 fusion.2
  292.8 0.0 all-reduce.4.cloned.1.call-update
  292.8 0.0 reduce-scatter.2.cloned.1.call-start
  292.9 3.0 convolution_convert_fusion
  295.9 0.0 reduce-scatter.2.cloned.1.call-update
  296.0 152.8 %all-reduce.4.cloned.1.call-done = bf16[1024,64]{0,1:T(8,128)(2,1)} async-done(((bf16[1024,64]{0,1:T(8,128)(2,1)}), bf16[1024,64]{0,1:T(8,128)(2,1)}) %all-reduce.4.cloned.1.call-update) | async-done | bytes 131088 | tf_op jit(solution)/shard_map/psum | solution.py:89
  448.8 0.8 dynamic-slice_convert_fusion
  449.6 0.7 copy.46
  450.3 66.2 %reduce-scatter.2.cloned.1.call-done = bf16[1792,64]{0,1:T(8,128)(2,1)} async-done(((bf16[1792,1024]{0,1:T(8,128)(2,1)}), bf16[1792,64]{0,1:T(8,128)(2,1)}) %reduce-scatter.2.cloned.1.call-update) | async-done | bytes 229392 | tf_op jit(solution)/shard_map/reduce_scatter | solution.py:96
  (21 shorter events, 0.1 us)
Async XLA Ops:
  7.2 8.2 %copy-start = (bf16[14,5,128,128]{3,2,1,0:T(8,128)(2,1)S(1)}, bf16[14,5,128,128]{3,2,1,0:T(8,128)(2,1)}, u32[]{:S(2)}) copy-start(bf16[14,5,128,128]{3,2,1,0:T(8,128)(2,1)} %param.18) | copy-start | bytes 6881284
  27.0 4.9 copy-start.3
  27.0 5.1 copy-start.5
  36.4 8.3 %collective-permute-start = (bf16[2,128,128]{2,1,0:T(8,128)(2,1)S(1)}, bf16[2,128,128]{2,1,0:T(8,128)(2,1)S(1)}, u32[]{:S(2)}, u32[]{:S(2)}) collective-permute-start(bf16[2,128,128]{2,1,0:T(8,128)(2,1)S(1)} %bitcast.58), channel_id=1, source_target_pairs={{0,16},{16,32},{32,48},{48,64},{64,80},{80,96},{96,112},{112,128},... | collective-permute-start | bytes 196616 | tf_op jit(solution)/shard_map/ppermute | solution.py:10
  39.9 6.4 %collective-permute-start.1 = (bf16[2,128,128]{2,1,0:T(8,128)(2,1)S(1)}, bf16[2,128,128]{2,1,0:T(8,128)(2,1)S(1)}, u32[]{:S(2)}, u32[]{:S(2)}) collective-permute-start(bf16[2,128,128]{2,1,0:T(8,128)(2,1)S(1)} %bitcast.59), channel_id=1, source_target_pairs={{16,0},{32,16},{48,32},{64,48},{80,64},{96,80},{112,96},{128,112},... | collective-permute-start | bytes 196616 | tf_op jit(solution)/shard_map/ppermute | solution.py:10
  50.5 11.2 %copy-start.2 = (bf16[32,64]{1,0:T(8,128)(2,1)S(1)}, bf16[32,64]{1,0:T(8,128)(2,1)}, u32[]{:S(2)}) copy-start(bf16[32,64]{1,0:T(8,128)(2,1)} %param.12) | copy-start | bytes 12292
  50.5 212.0 %copy-start.4 = (s32[448]{0:T(512)S(1)}, s32[448]{0:T(512)}, u32[]{:S(2)}) copy-start(s32[448]{0:T(512)} %param.21) | copy-start | bytes 5380
  50.5 212.5 %all-to-all-start = ((bf16[32,1792,64]{1,2,0:T(8,128)(2,1)}), bf16[32,1792,64]{1,2,0:T(8,128)(2,1)}, u32[]{:S(2)}, u32[]{:S(2)}) async-start(bf16[32,1792,64]{1,2,0:T(8,128)(2,1)} %stack.2), calls=%async_computation | async-start | bytes 14680064 | tf_op jit(solution)/shard_map/all_to_all | solution.py:75
  60.9 227.5 %all-gather.2.cloned.1.call-start = ((), (), s32[]{:S(2)}) async-start(), calls=%async_computation.2 | async-start | bytes 3899392 | tf_op jit(solution)/shard_map/all_gather | solution.py:82
  61.7 387.1 %all-reduce.4.cloned.1.call-start = ((), (), s32[]{:S(2)}) async-start(), calls=%async_computation.3 | async-start | bytes 262144 | tf_op jit(solution)/shard_map/psum | solution.py:89
  292.8 223.6 %copy-start.1 = (bf16[14,5,128,128]{3,2,1,0:T(8,128)(2,1)S(1)}, bf16[14,5,128,128]{3,2,1,0:T(8,128)(2,1)}, u32[]{:S(2)}) copy-start(bf16[14,5,128,128]{3,2,1,0:T(8,128)(2,1)} %param.18) | copy-start | bytes 6881284
  292.8 223.6 %reduce-scatter.2.cloned.1.call-start = ((), (), s32[]{:S(2)}) async-start(), calls=%async_computation.4 | async-start | bytes 3899392 | tf_op jit(solution)/shard_map/reduce_scatter | solution.py:96
Sparse Core Ops, SparseCore 0:
  63.9 49.0 all-gather.1
  293.0 155.7 all-reduce.3
  452.5 63.8 reduce-scatter.1
